TPU v7x, 128 devices: a whole 4x4x4 slice. The times are simulated.
128 devices in a mesh: row: 8 (over y, x_hi), col: 16 (over z, x_lo, core).
Axes of the slice: x: 4 (x_hi: 2, x_lo: 2; x = x_hi * 2 + x_lo), y: 4, z: 4, core: 2. Of those that a mesh axis runs over, the one named last changes fastest.
Arguments:
- activations: bfloat16 [2048, 8192], P('col', 'row'), may hold values from -6 to 6
- gradients: bfloat16 [2048, 8192], P('row', 'col'), may hold values from -6 to 6
- act_basis: bfloat16 [8192, 8192], P('row', 'col'), may hold values from -0.0625 to 0.0625
- grad_basis: bfloat16 [8192, 8192], P('col', 'row'), may hold values from -0.0625 to 0.0625
- lengths: int32 [8], replicated, may hold values from 1 to 512, 2048 in all
- seq_order: int32 [8], replicated, may hold values from 0 to 7, each once
Outputs:
- correction: float32 [8192, 8192], P('row', 'col')
Inputs may be any that keep to these rules, and one draw needn't show every extreme that they name: The lengths sum to 2048, and one of them is 512. `seq_order`: each sequence number appears once.
All inputs are finite; a program needn't handle non-finite values.
Results may differ from a plain program's by a relative error of at most 0.0029.
Values may be sent and summed in bfloat16 or wider, within the bound.
A program may use at most 64 MiB of HBM per device.

v0:
```python
import jax
import jax.numpy as jnp
from jax import lax
from jax.sharding import PartitionSpec as P

SEQS = 8
LMAX = 512
TOTAL = 2048


def shards(activations, gradients, act_basis, grad_basis, lengths, seq_order):
    act_part = jnp.dot(
        lax.all_gather(activations, "col", axis=0, tiled=True),
        act_basis,
        preferred_element_type=jnp.float32,
    )
    rot_acts = lax.psum(act_part, "row").astype(jnp.bfloat16)
    grad_part = jnp.dot(
        lax.all_gather(gradients, "row", axis=0, tiled=True),
        grad_basis,
        preferred_element_type=jnp.float32,
    )
    rot_grads = lax.psum(grad_part, "col").astype(jnp.bfloat16)
    in_cols = rot_acts.shape[1]
    out_cols = rot_grads.shape[1]
    padded_acts = jnp.concatenate([rot_acts, jnp.zeros((LMAX, in_cols), jnp.bfloat16)], axis=0)
    padded_grads = jnp.concatenate([rot_grads, jnp.zeros((LMAX, out_cols), jnp.bfloat16)], axis=0)
    select = (seq_order[:, None] == jnp.arange(SEQS, dtype=jnp.int32)[None, :]).astype(jnp.int32)
    ordered = jnp.sum(select * lengths[None, :], axis=1)
    starts = jnp.cumsum(ordered) - ordered

    def add_sequence(number, total):
        start = starts[number]
        window_acts = lax.dynamic_slice_in_dim(padded_acts, start, LMAX, 0)
        window_grads = lax.dynamic_slice_in_dim(padded_grads, start, LMAX, 0)
        live_rows = (jnp.arange(LMAX, dtype=jnp.int32) < ordered[number]).astype(jnp.bfloat16)
        window_grads = window_grads * live_rows[:, None]
        tile = lax.dot_general(
            window_grads, window_acts, (((0,), (0,)), ((), ())), preferred_element_type=jnp.float32
        )
        return total + tile * tile

    summed = lax.fori_loop(0, SEQS, add_sequence, jnp.zeros((out_cols, in_cols), jnp.float32))
    return summed * (1.0 / TOTAL)


def solution(mesh):
    in_specs = (P("col", "row"), P("row", "col"), P("row", "col"), P("col", "row"), P(), P())
    out_specs = P("row", "col")
    return jax.shard_map(shards, mesh=mesh, in_specs=in_specs, out_specs=out_specs, check_vma=False)
```

profile of v0, /device:TPU:1, one launch (start us, length us, event | category | flops | bytes accessed | tf_op | source)
XLA Modules:
  0.0 509.3 jit_solution(5502785986752809621)
XLA Ops:
  6.5 0.7 all-gather.3.cloned.1.call-update
  7.3 0.7 all-gather.5.cloned.1.call-update
  8.0 0.9 select_reduce_fusion
  9.1 57.4 %all-gather.3.cloned.1.call-done = bf16[2048,512]{1,0:T(8,128)(2,1)} async-done(((bf16[256,512]{1,0:T(8,128)(2,1)}), bf16[2048,512]{1,0:T(8,128)(2,1)}) %all-gather.3.cloned.1.call-update) | async-done | bytes 2097168 | tf_op jit(solution)/shard_map/all_gather | solution.py:19
  66.4 7.2 %fusion.6 = f32[2048,1024]{1,0:T(8,128)} fusion(bf16[2048,512]{1,0:T(8,128)(2,1)} %all-gather.3.cloned.1.call-done, bf16[512,1024]{1,0:T(8,128)(2,1)S(1)} %copy-done), kind=kOutput, calls=%fused_computation.12 | convolution fusion | flops 2147483648 | bytes 11534336 | tf_op jit(solution)/shard_map/dot_general | solution.py:18
  73.6 194.9 %all-reduce.4 = bf16[2048,1024]{1,0:T(8,128)(2,1)} all-reduce(f32[2048,1024]{1,0:T(8,128)} %fusion.6), channel_id=1, replica_groups=mesh['row'=8,'col'=16] {'col'}, use_global_device_ids=true, to_apply=%region_3.0 | all-reduce | flops 2097152 | bytes 12582912 | tf_op jit(solution)/shard_map/psum | solution.py:23
  268.5 5.1 concatenate.6
  273.5 6.8 %fusion.7 = f32[2048,512]{1,0:T(8,128)} fusion(bf16[2048,1024]{1,0:T(8,128)(2,1)} %all-gather.5.cloned.1.call-done, bf16[1024,512]{1,0:T(8,128)(2,1)} %param.10), kind=kOutput, calls=%fused_computation.13 | convolution fusion | flops 2147483648 | bytes 9437184 | tf_op jit(solution)/shard_map/dot_general | solution.py:12
  280.3 167.1 %all-reduce.5 = bf16[2048,512]{1,0:T(8,128)(2,1)} all-reduce(f32[2048,512]{1,0:T(8,128)} %fusion.7), channel_id=1, replica_groups=mesh['row'=8,'col'=16] {'row'}, use_global_device_ids=true, to_apply=%region_2.0 | all-reduce | flops 1048576 | bytes 6291456 | tf_op jit(solution)/shard_map/psum | solution.py:17
  447.4 3.3 concatenate.7
  450.7 50.3 %while.14 = (s32[]{:T(128)}, f32[1024,512]{1,0:T(8,128)S(1)}, s32[8]{0:T(128)S(1)}, bf16[2560,1024]{1,0:T(8,128)(2,1)}, s32[8]{0:T(128)S(1)}, /*index=5*/bf16[25...) while((s32[]{:T(128)}, f32[1024,512]{1,0:T(8,128)S(1)}, s32[8]{0:T(128)S(1)}, ...), condition=%wide.region_5.6_spmd.clone, body=%wide.region_4.5_spmd.clone.sunk | while | flops 540541952 | bytes 5770916 | solution.py:43
  453.2 0.6 dynamic_slice.45
  453.8 0.6 fusion.17
  454.4 2.5 select_add_fusion.2
  459.5 0.6 dynamic_slice.45
  460.1 0.6 fusion.17
  460.7 2.5 select_add_fusion.2
  465.8 0.6 dynamic_slice.45
  466.4 0.6 fusion.17
  467.0 2.5 select_add_fusion.2
  472.1 0.6 dynamic_slice.45
  472.6 0.6 fusion.17
  473.3 2.5 select_add_fusion.2
  478.9 0.6 fusion.17
  479.6 2.5 select_add_fusion.2
  485.2 0.6 fusion.17
  485.9 2.5 select_add_fusion.2
  491.5 0.6 fusion.17
  492.2 2.5 select_add_fusion.2
  497.8 0.6 fusion.17
  498.5 2.5 select_add_fusion.2
  501.0 1.6 broadcast_multiply_fusion
  (20 shorter events, 7.3 us)
Async XLA Ops:
  6.5 59.9 %copy-start = (bf16[512,1024]{1,0:T(8,128)(2,1)S(1)}, bf16[512,1024]{1,0:T(8,128)(2,1)}, u32[]{:S(2)}) copy-start(bf16[512,1024]{1,0:T(8,128)(2,1)} %param.11) | copy-start | bytes 3145732
  6.5 59.9 %all-gather.3.cloned.1.call-start = ((), (), s32[]{:S(2)}) async-start(), calls=%async_computation | async-start | bytes 2359296 | tf_op jit(solution)/shard_map/all_gather | solution.py:19
  7.3 266.3 %all-gather.5.cloned.1.call-start = ((), (), s32[]{:S(2)}) async-start(), calls=%async_computation.1 | async-start | bytes 4456448 | tf_op jit(solution)/shard_map/all_gather | solution.py:13
Sparse Core Ops, SparseCore 0:
  9.7 56.6 all-gather.2
  68.1 48.7 all-gather.4
where the time goes:
time: 513 us; the launch traced here: 509 us
  blocking collectives  362 us (71%)
  waiting for transfers between devices  58.8 us (11%)
  matrix products  33.8 us (7%)
  local copies, waits for them, and re-layouts  17.7 us (3%)
  loops' own time  15.8 us (3%)
  between operations  13.4 us (3%)
  other arithmetic  7.78 us (2%)
    psum x1, blocking collectives, shards(): rot_grads = lax.psum(grad_part, 'col').astype(jnp.bfloat16)  195 us
    psum x1, blocking collectives, shards(): rot_acts = lax.psum(act_part, 'row').astype(jnp.bfloat16)  167 us
    all_gather x1, waiting for transfers between devices, shards(): lax.all_gather(gradients, 'row', axis=0, tiled=True)  57.4 us
    dot_general x8, matrix products, add_sequence(): lax.dot_general(window_grads, window_acts, (((0,), (0,)), ((), ())), pref...  19.9 us
    another operation x1, loops' own time, shards(): lax.fori_loop(0, SEQS, add_sequence, jnp.zeros((out_cols, in_cols), jnp.f...  15.8 us
  transfers between devices with their start and end apart: 2, of which 1 were waited for; matrix products, arithmetic and copies ran while one was open for 3% of the time, Pallas kernels for 0%

commit v1 on v0

v1 whole, which is shorter than its diff:
```python
import functools

import jax
import jax.numpy as jnp
from jax import lax
from jax.experimental import pallas as pl
from jax.experimental.pallas import tpu as pltpu
from jax.sharding import PartitionSpec as P

MESH = pl.DeviceIdType.MESH
SEQS = 8
TOTAL = 2048
PARTS = 2
SCALE = 2.0**28

BF16, F32 = jnp.bfloat16, jnp.float32


def encode(v):
    v = v * SCALE
    return (v * v * v).astype(BF16)


def decode(m):
    v = m.astype(F32)
    size = jnp.abs(v)
    root = jnp.exp2(jnp.log2(jnp.maximum(size, 1e-37)) * (1.0 / 3.0)) * (1.0 / SCALE)
    root = jnp.where(size > 1e-37, root, 0.0)
    return jnp.where(v < 0, -root, root)


class Place:
    def __init__(self, ring, pair, peer):
        self.ring, self.pair, self.peer = ring, pair, peer

    def to(self, dr=0, dx=0):
        return self.peer(lax.rem(self.ring + dr + 4, 4), lax.rem(self.pair + dx, 2))

    def index(self, dr=0, dx=0):
        return lax.rem(self.ring + dr + 4, 4) * 2 + lax.rem(self.pair + dx, 2)


def exchange_kernel(
    acts, grads, act_basis, grad_basis, out_a, out_g,
    ga, gg, ba, bg, pf_a, pf_g, ms_a, ms_g, ra_a, ra_g, rb_a, rb_g, mx_a, mx_g, rx_a, rx_g, fin_a, fin_g,
    send_sems, recv_sems, local_sems,
):
    row, col = lax.axis_index("row"), lax.axis_index("col")
    y, xh = row // 2, lax.rem(row, 2)
    z, xl, core = col // 4, lax.rem(col // 2, 2), lax.rem(col, 2)
    other = 1 - core
    along_z = Place(z, xl, lambda r, p: (row, r * 4 + p * 2 + core))
    along_y = Place(y, xh, lambda r, p: (r * 2 + p, col))
    sibling = (row, z * 4 + xl * 2 + other)

    copies, locals_, events = {}, [], []

    def send(name, src, dst, to):
        n = len(copies)
        copy = pltpu.make_async_remote_copy(
            src_ref=src, dst_ref=dst, send_sem=send_sems.at[n], recv_sem=recv_sems.at[n],
            device_id=to, device_id_type=MESH,
        )
        copies[name] = copy
        copy.start()

    def got(name):
        copies[name].wait_recv()

    def local(src, dst):
        copy = pltpu.make_async_copy(src, dst, local_sems.at[len(locals_)])
        locals_.append(copy)
        copy.start()
        return copy

    def at(time, step, *args):
        events.append((time, len(events), functools.partial(step, *args)))

    partners = [along_z.to(1), along_z.to(3), along_z.to(0, 1), along_y.to(1), along_y.to(3), along_y.to(0, 1), sibling]
    barrier = pltpu.get_barrier_semaphore()
    for partner in partners:
        pl.semaphore_signal(barrier, inc=1, device_id=partner, device_id_type=MESH)
    own_a = local(acts, ga.at[0, 0, core])
    own_g = local(grads, gg.at[0, 0, core])
    load_a = local(act_basis, ba)
    half_of = lambda who: pl.ds(pl.multiple_of(who * 512, 512), 512)
    load_g = local(grad_basis.at[:, half_of(core)], bg.at[core])
    pl.semaphore_wait(barrier, len(partners))

    chains = {
        "a": dict(mine=acts, g=ga, first=along_z, second=along_y, pf=pf_a, ms=ms_a, ra=ra_a, rb=rb_a, mx=mx_a, rx=rx_a, fin=fin_a),
        "g": dict(mine=grads, g=gg, first=along_y, second=along_z, pf=pf_g, ms=ms_g, ra=ra_g, rb=rb_g, mx=mx_g, rx=rx_g, fin=fin_g),
    }

    def first_sends(k):
        c = chains[k]
        mine, g, place = c["mine"], c["g"], c["first"]
        send(k + "10", mine, g.at[3, 0, core], place.to(1))
        send(k + "30", mine, g.at[1, 0, core], place.to(3))
        send(k + "01", mine, g.at[0, 1, core], place.to(0, 1))
        send(k + "s00", mine, g.at[0, 0, core], sibling)

    def swap(k, dr, dx):
        g = chains[k]["g"]
        send(f"{k}s{dr}{dx}", g.at[dr, dx, core], g.at[dr, dx, core], sibling)

    def half(k, h):
        rows = 64 if k == "a" else 128
        return pl.ds(h * rows, rows)

    def pass_on(k, dx):
        g, place = chains[k]["g"], chains[k]["first"]
        got(f"{k}1{dx}")
        send(f"{k}f1{dx}", g.at[3, dx, core, half(k, 0)], g.at[2, dx, core, half(k, 0)], place.to(1))
        got(f"{k}3{dx}")
        send(f"{k}f3{dx}", g.at[1, dx, core, half(k, 1)], g.at[2, dx, core, half(k, 1)], place.to(3))
        swap(k, 3, dx)
        swap(k, 1, dx)

    def partner_block(k):
        g, place = chains[k]["g"], chains[k]["first"]
        got(k + "01")
        send(k + "11", g.at[0, 1, core], g.at[3, 1, core], place.to(1))
        send(k + "31", g.at[0, 1, core], g.at[1, 1, core], place.to(3))
        swap(k, 0, 1)

    def opposite(k, dx):
        got(f"{k}f1{dx}")
        got(f"{k}f3{dx}")
        swap(k, 2, dx)

    def partial(k, dr, dx):
        c = chains[k]
        first, second, g = c["first"], c["second"], c["g"]
        block = first.index(dr, dx)
        part, h, i = block // 4, lax.rem(block // 2, 2), lax.rem(block, 2)

        def keep(value, base):
            for s in range(value.shape[0] // 32):
                o = base + s
                q = lax.rem(o // 2 - second.ring + 4, 4)
                x = lax.rem(o % 2 + second.pair, 2)
                piece = value[s * 32 : (s + 1) * 32]
                c["pf"][q, x, part, h, i] = piece
                c["ms"][q, x, part, h, i] = encode(piece)

        if k == "a":
            for n in range(2):
                keep(jnp.dot(g[dr, dx, n], ba[...], preferred_element_type=F32), 4 * n)
        else:
            for n in range(2):
                rows = pl.ds(n * 128, 128)
                value = jnp.dot(g[dr, dx, 0, rows], bg[0], preferred_element_type=F32)
                value += jnp.dot(g[dr, dx, 1, rows], bg[1], preferred_element_type=F32)
                keep(value, 4 * n)

    def block_pair(k, dr, dx):
        got(f"{k}s{dr}{dx}")
        partial(k, dr, dx)

    def both_sides(k, dx):
        got(f"{k}s3{dx}")
        got(f"{k}s1{dx}")

        @pl.loop(0, 2)
        def _(n):
            partial(k, 1 + 2 * n, dx)

    def part_of(k, t):
        return lax.rem(chains[k]["first"].ring // 2 + t, 2)

    def spread(k, t, x):
        c = chains[k]
        ms, ra, rb, place, p = c["ms"], c["ra"], c["rb"], c["second"], part_of(k, t)
        tag = f"{k}{t}{x}"
        send(tag + "a1", ms.at[2, x, p, 0], ra.at[x, p, 0], place.to(1))
        send(tag + "a3", ms.at[2, x, p, 1], ra.at[x, p, 1], place.to(3))
        send(tag + "b1", ms.at[1, x, p, 1], rb.at[x, p, 0, 1], place.to(1))
        send(tag + "b3", ms.at[3, x, p, 0], rb.at[x, p, 1, 0], place.to(3))

    def join(k, t, x):
        c = chains[k]
        ms, ra, rb, pf, place, p = c["ms"], c["ra"], c["rb"], c["pf"], c["second"], part_of(k, t)
        tag = f"{k}{t}{x}"
        got(tag + "a1")
        ms[1, x, p, 0] = encode(pf[1, x, p, 0] + decode(ra[x, p, 0]))
        send(tag + "c1", ms.at[1, x, p, 0], rb.at[x, p, 0, 0], place.to(1))
        got(tag + "a3")
        ms[3, x, p, 1] = encode(pf[3, x, p, 1] + decode(ra[x, p, 1]))
        send(tag + "c3", ms.at[3, x, p, 1], rb.at[x, p, 1, 1], place.to(3))

    def finish(k, t, x):
        c = chains[k]
        rb, pf, place, p = c["rb"], c["pf"], c["second"], part_of(k, t)
        tag = f"{k}{t}{x}"
        for n in ("b1", "b3", "c1", "c3"):
            got(tag + n)
        total = pf[0, x, p] + (decode(rb[x, p, 0]) + decode(rb[x, p, 1]))
        if x == 1:
            c["mx"][p] = encode(total)
            send(f"{k}{t}x", c["mx"].at[p], c["rx"].at[p], place.to(0, 1))
        else:
            pf[0, 0, p] = total

    def out_of(k):
        return out_a if k == "a" else out_g.at[core]

    def region(k, p, owner, h=None):
        if h is None:
            return out_of(k).at[p, :, :, owner]
        return out_of(k).at[p, h, :, owner]

    def rounded(k, t):
        c = chains[k]
        place, p, fin = c["second"], part_of(k, t), c["fin"]
        got(f"{k}{t}x")
        fin[p] = (c["pf"][0, 0, p] + decode(c["rx"][p])).astype(BF16)
        mine = region(k, p, place.index())
        tag = f"{k}{t}r"
        send(tag + "10", fin.at[p], mine, place.to(1))
        send(tag + "30", fin.at[p], mine, place.to(3))
        send(tag + "01", fin.at[p], mine, place.to(0, 1))
        if k == "g":
            send(tag + "s00", fin.at[p], mine, sibling)
        local(fin.at[p], mine)

    def share(k, t, dr, dx):
        if k == "g":
            there = region(k, part_of(k, t), chains[k]["second"].index(dr, dx))
            send(f"{k}{t}rs{dr}{dx}", there, there, sibling)

    def pass_rounded(k, t, dx):
        place, p = chains[k]["second"], part_of(k, t)
        tag = f"{k}{t}r"
        got(f"{tag}1{dx}")
        there = region(k, p, place.index(3, dx), 0)
        send(f"{tag}f1{dx}", there, there, place.to(1))
        got(f"{tag}3{dx}")
        there = region(k, p, place.index(1, dx), 1)
        send(f"{tag}f3{dx}", there, there, place.to(3))
        share(k, t, 3, dx)
        share(k, t, 1, dx)

    def partner_rounded(k, t):
        place, p = chains[k]["second"], part_of(k, t)
        tag = f"{k}{t}r"
        got(tag + "01")
        there = region(k, p, place.index(0, 1))
        send(tag + "11", there, there, place.to(1))
        send(tag + "31", there, there, place.to(3))
        share(k, t, 0, 1)

    def opposite_rounded(k, t, dx):
        tag = f"{k}{t}r"
        got(f"{tag}f1{dx}")
        got(f"{tag}f3{dx}")
        share(k, t, 2, dx)

    for k in "ga":
        at(0, first_sends, k)
    at(0.1, lambda: send("basis", grad_basis.at[:, half_of(other)], bg.at[core], sibling))

    def loaded():
        for copy in (own_a, own_g, load_a, load_g):
            copy.wait()
        got("basis")

    at(1.9, loaded)
    for k in "ga":
        at(2, block_pair, k, 0, 0)
        at(5, pass_on, k, 0)
        at(6, partner_block, k)
        at(7.5, both_sides, k, 0)
        at(8, block_pair, k, 0, 1)
        at(9, opposite, k, 0)
        at(10, pass_on, k, 1)
        at(11, block_pair, k, 2, 0)
        at(12, both_sides, k, 1)
        at(15, opposite, k, 1)
        at(17, block_pair, k, 2, 1)
        for t, start in ((0, 12.5), (1, 18)):
            at(start, spread, k, t, 1)
            at(start + 0.1, spread, k, t, 0)
            at(start + 3, join, k, t, 1)
            at(start + 4, join, k, t, 0)
            at(start + 7, finish, k, t, 1)
            at(start + 9, finish, k, t, 0)
            at(start + 10, rounded, k, t)
            at(start + 13, pass_rounded, k, t, 0)
            at(start + 13.5, partner_rounded, k, t)
            at(start + 15, opposite_rounded, k, t, 0)
            at(start + 16, pass_rounded, k, t, 1)
            at(start + 18, opposite_rounded, k, t, 1)
    for _, _, step in sorted(events, key=lambda e: e[:2]):
        step()
    for t in range(PARTS):
        for dr in range(4):
            for dx in range(2):
                got(f"g{t}rs{dr}{dx}")
    for copy in locals_[4:]:
        copy.wait()
    for copy in copies.values():
        copy.wait_send()


def rotate(acts, grads, act_basis, grad_basis):
    any_space = pl.BlockSpec(memory_space=pl.ANY)
    shape = (2, 2, 2, 8, 32, 512)
    per_chain = lambda *dims, dtype=BF16: [pltpu.VMEM(dims, dtype)] * 2
    return pl.pallas_call(
        exchange_kernel,
        out_shape=(jax.ShapeDtypeStruct(shape, BF16), jax.ShapeDtypeStruct((2,) + shape, BF16)),
        in_specs=[any_space] * 4,
        out_specs=(any_space, any_space),
        scratch_shapes=[
            pltpu.VMEM((4, 2, 2, 128, 1024), BF16),
            pltpu.VMEM((4, 2, 2, 256, 512), BF16),
            pltpu.VMEM((1024, 512), BF16),
            pltpu.VMEM((2, 512, 512), BF16),
            *per_chain(4, 2, 2, 2, 2, 32, 512, dtype=F32),
            *per_chain(4, 2, 2, 2, 2, 32, 512),
            *per_chain(2, 2, 2, 2, 32, 512),
            *per_chain(2, 2, 2, 2, 2, 32, 512),
            *per_chain(2, 2, 2, 32, 512),
            *per_chain(2, 2, 2, 32, 512),
            *per_chain(2, 2, 2, 32, 512),
            pltpu.SemaphoreType.DMA((160,)),
            pltpu.SemaphoreType.DMA((160,)),
            pltpu.SemaphoreType.DMA((16,)),
        ],
        compiler_params=pltpu.CompilerParams(collective_id=0, has_side_effects=True, vmem_limit_bytes=60 << 20),
        cost_estimate=pl.CostEstimate(flops=4 * 2048 * 1024 * 512, bytes_accessed=10 << 20, transcendentals=0),
    )(acts, grads, act_basis, grad_basis)


CHUNK = 256


def tiles_kernel(lengths, order, ra, rg, out, tile):
    out[...] = jnp.zeros_like(out)

    @pl.loop(0, SEQS, init_carry=jnp.int32(0))
    def _(k, start):
        end = start + lengths[order[k]]
        low, high = start // CHUNK, (end + CHUNK - 1) // CHUNK
        tile[...] = jnp.zeros_like(tile)

        @pl.loop(low, high)
        def _(n):
            rows = pl.ds(pl.multiple_of(n * CHUNK, CHUNK), CHUNK)
            at = n * CHUNK + lax.broadcasted_iota(jnp.int32, (CHUNK, 1), 0)
            live = (at >= start) & (at < end)
            a = jnp.where(live, ra[rows], 0)
            for h in range(2):
                tile[h * 512 : (h + 1) * 512] += lax.dot_general(
                    rg[h, rows], a, (((0,), (0,)), ((), ())), preferred_element_type=F32
                )

        out[...] += tile[...] * tile[...]
        return end

    out[...] = out[...] * (1.0 / TOTAL)


def tiles(lengths, order, ra, rg):
    smem, vmem = pl.BlockSpec(memory_space=pltpu.SMEM), pl.BlockSpec(memory_space=pltpu.VMEM)
    return pl.pallas_call(
        tiles_kernel,
        out_shape=jax.ShapeDtypeStruct((1024, 512), F32),
        in_specs=[smem, smem, vmem, vmem],
        out_specs=vmem,
        scratch_shapes=[pltpu.VMEM((1024, 512), F32)],
        compiler_params=pltpu.CompilerParams(vmem_limit_bytes=40 << 20),
    )(lengths, order, ra, rg)


def shards(activations, gradients, act_basis, grad_basis, lengths, seq_order):
    ra, rg = rotate(activations, gradients, act_basis, grad_basis)
    return tiles(lengths, seq_order, ra.reshape(2048, 512), rg.reshape(2, 2048, 512))


def solution(mesh):
    in_specs = (P("col", "row"), P("row", "col"), P("row", "col"), P("col", "row"), P(), P())
    return jax.shard_map(shards, mesh=mesh, in_specs=in_specs, out_specs=P("row", "col"), check_vma=False)
```

time: 513 us -> 98.2 us (0.19)
  blocking collectives: 362 us -> 0 us
  Pallas kernels: 0 us -> 94.3 us
  waiting for transfers between devices: 58.8 us -> 0 us
  matrix products: 33.8 us -> 0 us
  loops' own time: 15.8 us -> 0 us
  local copies, waits for them, and re-layouts: 17.7 us -> 3.78 us
  between operations: 13.4 us -> 0.04 us
  other arithmetic: 7.78 us -> 0 us
    psum x2 -> x0, blocking collectives: 362 us -> none  [the longest x1 195 us: shards(): rot_grads = lax.psum(grad_part, 'col').astype(jnp.bfloat16)]
    pallas_call x0 -> x2, Pallas kernels: none -> 94.3 us  [the longest x1 82.4 us: rotate(): pl.pallas_call(exchange_kernel, out_shape=(jax.ShapeDtypeStruct(shape, BF...]
    all_gather x2 -> x0, waiting for transfers between devices: 57.4 us -> none  [the longest x1 57.4 us: shards(): lax.all_gather(gradients, 'row', axis=0, tiled=True)]
    dot_general x10 -> x0, matrix products: 33.8 us -> none  [the longest x8 19.9 us: add_sequence(): lax.dot_general(window_grads, window_acts, (((0,), (0,)), ((), ())), pref...]
    another operation x1 -> x0, loops' own time: 15.8 us -> none  [shards(): lax.fori_loop(0, SEQS, add_sequence, jnp.zeros((out_cols, in_cols), jnp.f...]
    dynamic_slice x16 -> x0, local copies, waits for them, and re-layouts: 9.39 us -> none  [the longest x8 4.71 us: add_sequence(): ordered[number]]
    concatenate x2 -> x0, local copies, waits for them, and re-layouts: 8.35 us -> none  [the longest x1 5.08 us: shards(): jnp.concatenate([rot_grads, jnp.zeros((LMAX, out_cols), jnp.bfloat16)], a...]
    convert_element_type x8 -> x0, other arithmetic: 5.18 us -> none  [add_sequence(): (jnp.arange(LMAX, dtype=jnp.int32) < ordered[number]).astype(jnp.bfloat16)]
  transfers between devices with their start and end apart: 2 -> 0, of which waited for: 1 -> 0; matrix products, arithmetic and copies ran while one was open for 3% -> 0% of each run, Pallas kernels for 0% -> 0%
where the time goes in v1:
time: 98.2 us; the launch traced here: 98.1 us
  Pallas kernels  94.3 us (96%)
  local copies, waits for them, and re-layouts  3.78 us (4%)
    pallas_call x1, Pallas kernels, rotate(): pl.pallas_call(exchange_kernel, out_shape=(jax.ShapeDtypeStruct(shape, BF...  82.4 us
    pallas_call x1, Pallas kernels, tiles(): pl.pallas_call(tiles_kernel, out_shape=jax.ShapeDtypeStruct((1024, 512),...  11.9 us
    unnamed x8, local copies, waits for them, and re-layouts  3.78 us

profile of v1, /device:TPU:1, one launch (start us, length us, event | category | flops | bytes accessed | tf_op | source)
XLA Modules:
  0.0 98.1 jit_solution(16940479142070166711)
XLA Ops:
  0.0 0.0 copy-start.3
  0.0 0.0 copy-start.2
  0.0 82.4 %shard_map.64 = (bf16[2,2,2,8,32,512]{5,4,3,2,1,0:T(8,128)(2,1)}, bf16[2,2,2,2,8,32,512]{6,5,4,3,2,1,0:T(8,128)(2,1)}) custom-call(bf16[128,1024]{1,0:T(8,128)(2,1)} %acts.1, bf16[256,512]{1,0:T(8,128)(2,1)} %grads.1, bf16[1024,512]{1,0:T(8,128)(2,1)} %act_basis.1, bf16[512,1024]{1,0:T(8,128)(2,1)} %grad_basis.1), custom_call_target="tpu_custom_call" | custom-call | flops 4294967296 | bytes 10485760 | tf_op jit(solution)/shard_map/pallas_call | solution.py:310
  82.4 0.0 copy-done.3
  82.4 0.0 copy-done.2
  82.4 0.0 copy-start
  82.4 2.2 %copy-done = bf16[2,2,2,2,8,32,512]{6,5,4,3,2,1,0:T(8,128)(2,1)S(1)} copy-done((bf16[2,2,2,2,8,32,512]{6,5,4,3,2,1,0:T(8,128)(2,1)S(1)}, bf16[2,2,2,2,8,32,512]{6,5,4,3,2,1,0:T(8,128)(2,1)}, u32[]{:S(2)}) %copy-start) | copy-done | bytes 4194328
  84.6 0.0 copy-start.1
  84.6 1.6 %copy-done.1 = bf16[2,2,2,8,32,512]{5,4,3,2,1,0:T(8,128)(2,1)S(1)} copy-done((bf16[2,2,2,8,32,512]{5,4,3,2,1,0:T(8,128)(2,1)S(1)}, bf16[2,2,2,8,32,512]{5,4,3,2,1,0:T(8,128)(2,1)}, u32[]{:S(2)}) %copy-start.1) | copy-done | bytes 2097176
  86.2 11.9 %shard_map.65 = f32[1024,512]{1,0:T(8,128)} custom-call(s32[8]{0:T(128)S(1)} %copy-done.2, s32[8]{0:T(128)S(1)} %copy-done.3, bf16[2048,512]{1,0:T(8,128)(2,1)S(1)} %bitcast.3, bf16[2,2048,512]{2,1,0:T(8,128)(2,1)S(1)} %bitcast.2), custom_call_target="tpu_custom_call" | custom-call | tf_op jit(solution)/shard_map/pallas_call | solution.py:367
Async XLA Ops:
  0.0 82.4 %copy-start.3 = (s32[8]{0:T(128)S(1)}, s32[8]{0:T(128)}, u32[]{:S(2)}) copy-start(s32[8]{0:T(128)} %order.1) | copy-start | bytes 100
  0.0 82.4 %copy-start.2 = (s32[8]{0:T(128)S(1)}, s32[8]{0:T(128)}, u32[]{:S(2)}) copy-start(s32[8]{0:T(128)} %lengths.1) | copy-start | bytes 100
  82.4 2.2 %copy-start = (bf16[2,2,2,2,8,32,512]{6,5,4,3,2,1,0:T(8,128)(2,1)S(1)}, bf16[2,2,2,2,8,32,512]{6,5,4,3,2,1,0:T(8,128)(2,1)}, u32[]{:S(2)}) copy-start(bf16[2,2,2,2,8,32,512]{6,5,4,3,2,1,0:T(8,128)(2,1)} %get-tuple-element.8) | copy-start | bytes 12582916
  84.6 1.6 %copy-start.1 = (bf16[2,2,2,8,32,512]{5,4,3,2,1,0:T(8,128)(2,1)S(1)}, bf16[2,2,2,8,32,512]{5,4,3,2,1,0:T(8,128)(2,1)}, u32[]{:S(2)}) copy-start(bf16[2,2,2,8,32,512]{5,4,3,2,1,0:T(8,128)(2,1)} %get-tuple-element.7) | copy-start | bytes 6291460
